TPU v7x, 32 devices: a whole 2x2x4 slice. The times are simulated.
32 devices in a mesh: grp: 2 (over x), chan: 16 (over z, y, core).
Axes of the slice: x: 2, y: 2, z: 4, core: 2. Of those that a mesh axis runs over, the one named last changes fastest.
Arguments:
- voltages: bfloat16 [4096, 64, 512], P('chan', 'grp'), parts along dimension 1, may hold values from -6 to 6
- exponents: int32 [64], P('grp'), parts along dimension 0, may hold values from 0 to 2, as said below
- pairs: int32 [128, 2], replicated, may hold values from 0 to 31, as said below
Outputs:
- visibilities: bfloat16 [64, 128, 2, 128, 128], P(('grp', 'chan')), parts along dimension 0
There are 2 independent parts, one for each index of `grp`. A program takes and returns all parts, laid end to end along the dimension named above; an argument that names none is the same for every part. Nothing has to cross between parts.
Inputs may be any that keep to these rules, and one draw needn't show every extreme that they name: exponents are whole numbers. The 128 pairs are distinct and each has first member at most its second.
All inputs are finite; a program needn't handle non-finite values.
Results may differ from a plain program's by a relative error of at most 0.001.
Values may be sent and summed in bfloat16 or wider, within the bound.
A program may use at most 192 MiB of HBM per device.

v0:
```python
import jax
import jax.numpy as jnp
from jax import lax
from jax.sharding import PartitionSpec as P

PANEL = 128
NT = 256


def correlate_plane(plane, pairs):
    width = plane.shape[1]
    half = width // 2
    count = plane.shape[0] // PANEL
    panels = plane.reshape(count, PANEL, width)
    group_size = 32
    groups = pairs.reshape(-1, group_size, 2)
    labels = jnp.arange(count, dtype=jnp.int32)

    def select(which):
        onehot = (which[:, None] == labels[None, :]).astype(jnp.bfloat16)
        picked = jnp.einsum("kn,nix->kix", onehot, panels, preferred_element_type=jnp.float32)
        return picked.astype(jnp.bfloat16).reshape(group_size, PANEL, 2, half)

    def one_group(chosen):
        left = select(chosen[:, 0])
        right = select(chosen[:, 1])
        quads = jnp.einsum("kiat,kjbt->kabij", left, right, preferred_element_type=jnp.float32)
        real_part = quads[:, 0, 0] + quads[:, 1, 1]
        imag_part = quads[:, 1, 0] - quads[:, 0, 1]
        return jnp.stack([real_part, imag_part], axis=1)

    return lax.map(one_group, groups).reshape(-1, 2, PANEL, PANEL)


def correlate_channels(turned, pairs):

    def one_channel(plane):
        return correlate_plane(plane, pairs)

    return lax.map(one_channel, jnp.moveaxis(turned, 1, 0))


def input_power(turned):
    wide = turned.astype(jnp.float32)
    return jnp.sum(wide * wide, axis=(1, 2))


def on_device(voltages, exponents, pairs):
    gain = jnp.exp2(-exponents.astype(jnp.float32)).astype(jnp.bfloat16)
    scaled = voltages * gain[None, :, None]
    total_samples = exponents.shape[0] * NT
    power = lax.all_gather(input_power(scaled), "chan", axis=0, tiled=True)
    turned = lax.all_to_all(scaled, "chan", split_axis=1, concat_axis=0, tiled=True)
    raw = correlate_channels(turned, pairs)
    mean_power = power / total_samples
    rows = mean_power.reshape(-1, PANEL)
    left_power = jnp.take(rows, pairs[:, 0], axis=0)
    right_power = jnp.take(rows, pairs[:, 1], axis=0)
    denom = jnp.sqrt(NT * left_power[:, :, None] * right_power[:, None, :])
    return (raw / denom[None, :, None, :, :]).astype(jnp.bfloat16)


def solution(mesh):
    return jax.shard_map(
        on_device,
        mesh=mesh,
        in_specs=(P("chan", "grp", None), P("grp"), P()),
        out_specs=P(("grp", "chan"), None, None, None, None),
        check_vma=False,
    )
```

profile of v0, /device:TPU:11, one launch (start us, length us, event | category | flops | bytes accessed | tf_op | source)
XLA Modules:
  0.0 683.6 jit_solution(13939410700513925443)
XLA Ops:
  0.7 9.6 %multiply_reduce_fusion = (f32[256]{0:T(256)S(1)}, bf16[256,32,512]{2,0,1:T(8,128)(2,1)}) fusion(bf16[32]{0:T(256)(128)(2,1)S(1)} %exponential_convert_fusion, bf16[256,32,512]{2,1,0:T(8,128)(2,1)} %param.9), kind=kLoop, calls=%fused_computation.29 | loop fusion | flops 16776960 | bytes 16778304 | tf_op jit(solution)/shard_map/reduce_sum | solution.py:45
  10.3 6.7 all-to-all-start
  17.1 192.6 %all-gather = f32[16,1,256]{2,1,0:T(1,128)S(1)} all-gather(f32[1,1,256]{2,1,0:T(1,128)S(1)} %bitcast.99), channel_id=1, replica_groups=mesh['grp'=2,'chan'=16] {'chan'}, dimensions={0}, use_global_device_ids=true | all-gather | bytes 17408 | tf_op jit(solution)/shard_map/all_gather | solution.py:52
  215.7 7.5 %copy.26 = bf16[16,256,2,512]{3,1,0,2:T(8,128)(2,1)} copy(bf16[16,256,2,512]{3,1,2,0:T(8,128)(2,1)} %bitcast.3) | data formatting | bytes 16777216 | tf_op jit(solution)/shard_map/all_to_all | solution.py:53
  223.2 440.5 %while.23 = (s32[]{:T(128)}, f32[2,128,2,128,128]{4,3,2,1,0:T(8,128)}, s32[128,2]{0,1:T(2,128)S(1)}, bf16[2,4096,512]{2,1,0:T(8,128)(2,1)}, s32[]{:T(128)}, /*index=5*/s32[]{:T(128)}, s32[]{:T(128)}) while((s32[]{:T(128)}, f32[2,128,2,128,128]{4,3,2,1,0:T(8,128)}, s32[128,2]{0,1:T(2,128)S(1)}, bf16[2,4096,512]{2,1,0:T(8,128)(2,1)}, s32[]{:T(128)}, ...), condition=%wide.region_3.4_spmd, body=%wide.region_0.3_spmd.sunk | while | flops 1348470784 | bytes 138415600 | solution.py:40
  230.2 201.7 %while.24 = (s32[]{:T(128)}, f32[4,32,2,128,128]{4,3,2,1,0:T(8,128)}, s32[4,32,2]{1,0,2:T(4,128)S(1)}, bf16[32,128,512]{2,0,1:T(8,128)(2,1)}, s32[]{:T(128)}) while((s32[]{:T(128)}, f32[4,32,2,128,128]{4,3,2,1,0:T(8,128)}, s32[4,32,2]{1,0,2:T(4,128)S(1)}, bf16[32,128,512]{2,0,1:T(8,128)(2,1)}, s32[]{:T(128)}) %tuple.52), condition=%wide.region_2.2_spmd.clone.clone, body=%wide.region_1.1_spmd.clone.clone.sunk | while | flops 1348470784 | bytes 88081744 | solution.py:32
  230.2 5.4 convolution_convert_fusion.4
  235.6 6.9 %reshape.106 = bf16[32,128,2,256]{3,2,0,1:T(2,128)(2,1)} reshape(bf16[32,128,512]{2,0,1:T(8,128)(2,1)} %convolution_convert_fusion.4) | data formatting | bytes 8388608 | tf_op jit(solution)/shard_map/while/body/eval_jaxpr/while/body/eval_jaxpr/reshape | solution.py:22
  248.0 6.9 %reshape.107 = bf16[32,128,2,256]{3,2,0,1:T(2,128)(2,1)} reshape(bf16[32,128,512]{2,0,1:T(8,128)(2,1)} %convolution_convert_fusion.5) | data formatting | bytes 8388608 | tf_op jit(solution)/shard_map/while/body/eval_jaxpr/while/body/eval_jaxpr/reshape | solution.py:22
  254.9 12.5 %fusion.36 = f32[32,2,2,128,128]{3,4,1,2,0:T(8,128)S(1)} fusion(bf16[32,128,2,256,1]{3,2,0,1,4:T(2,128)(2,1)} %bitcast.91, bf16[32,128,2,256,1]{3,2,0,1,4:T(2,128)(2,1)} %bitcast.92), kind=kOutput, calls=%fused_computation.7.clone.1 | convolution fusion | flops 1073741824 | bytes 16777216 | tf_op jit(solution)/shard_map/while/body/eval_jaxpr/while/body/eval_jaxpr/kiat,kjbt->kabij/dot_general | solution.py:27
  270.3 5.6 copy.55
  280.6 5.4 convolution_convert_fusion.4
  286.0 6.9 %reshape.106 = bf16[32,128,2,256]{3,2,0,1:T(2,128)(2,1)} reshape(bf16[32,128,512]{2,0,1:T(8,128)(2,1)} %convolution_convert_fusion.4) | data formatting | bytes 8388608 | tf_op jit(solution)/shard_map/while/body/eval_jaxpr/while/body/eval_jaxpr/reshape | solution.py:22
  293.0 5.4 convolution_convert_fusion.5
  298.4 6.9 %reshape.107 = bf16[32,128,2,256]{3,2,0,1:T(2,128)(2,1)} reshape(bf16[32,128,512]{2,0,1:T(8,128)(2,1)} %convolution_convert_fusion.5) | data formatting | bytes 8388608 | tf_op jit(solution)/shard_map/while/body/eval_jaxpr/while/body/eval_jaxpr/reshape | solution.py:22
  305.3 12.5 %fusion.36 = f32[32,2,2,128,128]{3,4,1,2,0:T(8,128)S(1)} fusion(bf16[32,128,2,256,1]{3,2,0,1,4:T(2,128)(2,1)} %bitcast.91, bf16[32,128,2,256,1]{3,2,0,1,4:T(2,128)(2,1)} %bitcast.92), kind=kOutput, calls=%fused_computation.7.clone.1 | convolution fusion | flops 1073741824 | bytes 16777216 | tf_op jit(solution)/shard_map/while/body/eval_jaxpr/while/body/eval_jaxpr/kiat,kjbt->kabij/dot_general | solution.py:27
  320.7 5.6 copy.55
  336.4 6.9 %reshape.106 = bf16[32,128,2,256]{3,2,0,1:T(2,128)(2,1)} reshape(bf16[32,128,512]{2,0,1:T(8,128)(2,1)} %convolution_convert_fusion.4) | data formatting | bytes 8388608 | tf_op jit(solution)/shard_map/while/body/eval_jaxpr/while/body/eval_jaxpr/reshape | solution.py:22
  343.4 5.4 convolution_convert_fusion.5
  348.8 6.9 %reshape.107 = bf16[32,128,2,256]{3,2,0,1:T(2,128)(2,1)} reshape(bf16[32,128,512]{2,0,1:T(8,128)(2,1)} %convolution_convert_fusion.5) | data formatting | bytes 8388608 | tf_op jit(solution)/shard_map/while/body/eval_jaxpr/while/body/eval_jaxpr/reshape | solution.py:22
  355.7 12.5 %fusion.36 = f32[32,2,2,128,128]{3,4,1,2,0:T(8,128)S(1)} fusion(bf16[32,128,2,256,1]{3,2,0,1,4:T(2,128)(2,1)} %bitcast.91, bf16[32,128,2,256,1]{3,2,0,1,4:T(2,128)(2,1)} %bitcast.92), kind=kOutput, calls=%fused_computation.7.clone.1 | convolution fusion | flops 1073741824 | bytes 16777216 | tf_op jit(solution)/shard_map/while/body/eval_jaxpr/while/body/eval_jaxpr/kiat,kjbt->kabij/dot_general | solution.py:27
  371.1 5.6 copy.55
  381.4 5.4 convolution_convert_fusion.4
  386.9 6.9 %reshape.106 = bf16[32,128,2,256]{3,2,0,1:T(2,128)(2,1)} reshape(bf16[32,128,512]{2,0,1:T(8,128)(2,1)} %convolution_convert_fusion.4) | data formatting | bytes 8388608 | tf_op jit(solution)/shard_map/while/body/eval_jaxpr/while/body/eval_jaxpr/reshape | solution.py:22
  393.8 5.4 convolution_convert_fusion.5
  399.2 6.9 %reshape.107 = bf16[32,128,2,256]{3,2,0,1:T(2,128)(2,1)} reshape(bf16[32,128,512]{2,0,1:T(8,128)(2,1)} %convolution_convert_fusion.5) | data formatting | bytes 8388608 | tf_op jit(solution)/shard_map/while/body/eval_jaxpr/while/body/eval_jaxpr/reshape | solution.py:22
  406.1 12.5 %fusion.36 = f32[32,2,2,128,128]{3,4,1,2,0:T(8,128)S(1)} fusion(bf16[32,128,2,256,1]{3,2,0,1,4:T(2,128)(2,1)} %bitcast.91, bf16[32,128,2,256,1]{3,2,0,1,4:T(2,128)(2,1)} %bitcast.92), kind=kOutput, calls=%fused_computation.7.clone.1 | convolution fusion | flops 1073741824 | bytes 16777216 | tf_op jit(solution)/shard_map/while/body/eval_jaxpr/while/body/eval_jaxpr/kiat,kjbt->kabij/dot_general | solution.py:27
  421.5 5.6 copy.55
  431.8 11.6 %bitcast_dynamic-update-slice_fusion.2 = f32[2,128,2,128,128]{4,3,2,1,0:T(8,128)} fusion(f32[2,128,2,128,128]{4,3,2,1,0:T(8,128)} %get-tuple-element.207, s32[]{:T(128)S(6)} %copy.66, f32[1,128,2,128,128]{4,3,2,1,0:T(8,128)} %bitcast.93), kind=kLoop, calls=%fused_computation.26.clone.1 | loop fusion | bytes 33554436 | tf_op jit(solution)/shard_map/while/body/jit(dynamic_update_index_in_dim)/dynamic_update_slice | solution.py:40
  450.5 201.6 %while.24 = (s32[]{:T(128)}, f32[4,32,2,128,128]{4,3,2,1,0:T(8,128)}, s32[4,32,2]{1,0,2:T(4,128)S(1)}, bf16[32,128,512]{2,0,1:T(8,128)(2,1)}, s32[]{:T(128)}) while((s32[]{:T(128)}, f32[4,32,2,128,128]{4,3,2,1,0:T(8,128)}, s32[4,32,2]{1,0,2:T(4,128)S(1)}, bf16[32,128,512]{2,0,1:T(8,128)(2,1)}, s32[]{:T(128)}) %tuple.52), condition=%wide.region_2.2_spmd.clone.clone, body=%wide.region_1.1_spmd.clone.clone.sunk | while | flops 1348470784 | bytes 88081744 | solution.py:32
  455.9 6.9 %reshape.106 = bf16[32,128,2,256]{3,2,0,1:T(2,128)(2,1)} reshape(bf16[32,128,512]{2,0,1:T(8,128)(2,1)} %convolution_convert_fusion.4) | data formatting | bytes 8388608 | tf_op jit(solution)/shard_map/while/body/eval_jaxpr/while/body/eval_jaxpr/reshape | solution.py:22
  468.3 6.9 %reshape.107 = bf16[32,128,2,256]{3,2,0,1:T(2,128)(2,1)} reshape(bf16[32,128,512]{2,0,1:T(8,128)(2,1)} %convolution_convert_fusion.5) | data formatting | bytes 8388608 | tf_op jit(solution)/shard_map/while/body/eval_jaxpr/while/body/eval_jaxpr/reshape | solution.py:22
  475.1 12.5 %fusion.36 = f32[32,2,2,128,128]{3,4,1,2,0:T(8,128)S(1)} fusion(bf16[32,128,2,256,1]{3,2,0,1,4:T(2,128)(2,1)} %bitcast.91, bf16[32,128,2,256,1]{3,2,0,1,4:T(2,128)(2,1)} %bitcast.92), kind=kOutput, calls=%fused_computation.7.clone.1 | convolution fusion | flops 1073741824 | bytes 16777216 | tf_op jit(solution)/shard_map/while/body/eval_jaxpr/while/body/eval_jaxpr/kiat,kjbt->kabij/dot_general | solution.py:27
  490.5 5.6 copy.55
  506.3 6.9 %reshape.106 = bf16[32,128,2,256]{3,2,0,1:T(2,128)(2,1)} reshape(bf16[32,128,512]{2,0,1:T(8,128)(2,1)} %convolution_convert_fusion.4) | data formatting | bytes 8388608 | tf_op jit(solution)/shard_map/while/body/eval_jaxpr/while/body/eval_jaxpr/reshape | solution.py:22
  518.7 6.9 %reshape.107 = bf16[32,128,2,256]{3,2,0,1:T(2,128)(2,1)} reshape(bf16[32,128,512]{2,0,1:T(8,128)(2,1)} %convolution_convert_fusion.5) | data formatting | bytes 8388608 | tf_op jit(solution)/shard_map/while/body/eval_jaxpr/while/body/eval_jaxpr/reshape | solution.py:22
  525.5 12.5 %fusion.36 = f32[32,2,2,128,128]{3,4,1,2,0:T(8,128)S(1)} fusion(bf16[32,128,2,256,1]{3,2,0,1,4:T(2,128)(2,1)} %bitcast.91, bf16[32,128,2,256,1]{3,2,0,1,4:T(2,128)(2,1)} %bitcast.92), kind=kOutput, calls=%fused_computation.7.clone.1 | convolution fusion | flops 1073741824 | bytes 16777216 | tf_op jit(solution)/shard_map/while/body/eval_jaxpr/while/body/eval_jaxpr/kiat,kjbt->kabij/dot_general | solution.py:27
  540.9 5.6 copy.55
  556.7 6.9 %reshape.106 = bf16[32,128,2,256]{3,2,0,1:T(2,128)(2,1)} reshape(bf16[32,128,512]{2,0,1:T(8,128)(2,1)} %convolution_convert_fusion.4) | data formatting | bytes 8388608 | tf_op jit(solution)/shard_map/while/body/eval_jaxpr/while/body/eval_jaxpr/reshape | solution.py:22
  569.1 6.9 %reshape.107 = bf16[32,128,2,256]{3,2,0,1:T(2,128)(2,1)} reshape(bf16[32,128,512]{2,0,1:T(8,128)(2,1)} %convolution_convert_fusion.5) | data formatting | bytes 8388608 | tf_op jit(solution)/shard_map/while/body/eval_jaxpr/while/body/eval_jaxpr/reshape | solution.py:22
  575.9 12.5 %fusion.36 = f32[32,2,2,128,128]{3,4,1,2,0:T(8,128)S(1)} fusion(bf16[32,128,2,256,1]{3,2,0,1,4:T(2,128)(2,1)} %bitcast.91, bf16[32,128,2,256,1]{3,2,0,1,4:T(2,128)(2,1)} %bitcast.92), kind=kOutput, calls=%fused_computation.7.clone.1 | convolution fusion | flops 1073741824 | bytes 16777216 | tf_op jit(solution)/shard_map/while/body/eval_jaxpr/while/body/eval_jaxpr/kiat,kjbt->kabij/dot_general | solution.py:27
  591.3 5.6 copy.55
  607.1 6.9 %reshape.106 = bf16[32,128,2,256]{3,2,0,1:T(2,128)(2,1)} reshape(bf16[32,128,512]{2,0,1:T(8,128)(2,1)} %convolution_convert_fusion.4) | data formatting | bytes 8388608 | tf_op jit(solution)/shard_map/while/body/eval_jaxpr/while/body/eval_jaxpr/reshape | solution.py:22
  619.5 6.9 %reshape.107 = bf16[32,128,2,256]{3,2,0,1:T(2,128)(2,1)} reshape(bf16[32,128,512]{2,0,1:T(8,128)(2,1)} %convolution_convert_fusion.5) | data formatting | bytes 8388608 | tf_op jit(solution)/shard_map/while/body/eval_jaxpr/while/body/eval_jaxpr/reshape | solution.py:22
  626.3 12.5 %fusion.36 = f32[32,2,2,128,128]{3,4,1,2,0:T(8,128)S(1)} fusion(bf16[32,128,2,256,1]{3,2,0,1,4:T(2,128)(2,1)} %bitcast.91, bf16[32,128,2,256,1]{3,2,0,1,4:T(2,128)(2,1)} %bitcast.92), kind=kOutput, calls=%fused_computation.7.clone.1 | convolution fusion | flops 1073741824 | bytes 16777216 | tf_op jit(solution)/shard_map/while/body/eval_jaxpr/while/body/eval_jaxpr/kiat,kjbt->kabij/dot_general | solution.py:27
  641.7 5.6 copy.55
  652.1 11.6 %bitcast_dynamic-update-slice_fusion.2 = f32[2,128,2,128,128]{4,3,2,1,0:T(8,128)} fusion(f32[2,128,2,128,128]{4,3,2,1,0:T(8,128)} %get-tuple-element.207, s32[]{:T(128)S(6)} %copy.66, f32[1,128,2,128,128]{4,3,2,1,0:T(8,128)} %bitcast.93), kind=kLoop, calls=%fused_computation.26.clone.1 | loop fusion | bytes 33554436 | tf_op jit(solution)/shard_map/while/body/jit(dynamic_update_index_in_dim)/dynamic_update_slice | solution.py:40
  663.7 19.9 %divide_convert_fusion = bf16[2,128,2,128,128]{4,3,2,1,0:T(8,128)(2,1)} fusion(f32[2,128,2,128,128]{4,3,2,1,0:T(8,128)} %get-tuple-element.58, f32[128,128,128]{2,1,0:T(8,128)} %multiply_sqrt_fusion), kind=kLoop, calls=%fused_computation.28 | loop fusion | flops 16777216 | bytes 58720256 | tf_op jit(solution)/shard_map/convert_element_type | solution.py:60
  (79 shorter events, 135.5 us)
Async XLA Ops:
  10.3 199.4 %copy-start = (s32[128,2]{0,1:T(2,128)S(1)}, s32[128,2]{0,1:T(2,128)}, u32[]{:S(2)}) copy-start(s32[128,2]{0,1:T(2,128)} %param.11) | copy-start | bytes 3076
  10.3 205.4 %all-to-all-start = ((bf16[256,32,512]{2,0,1:T(8,128)(2,1)}), bf16[256,32,512]{2,0,1:T(8,128)(2,1)}, u32[]{:S(2)}, u32[]{:S(2)}) async-start(bf16[256,32,512]{2,0,1:T(8,128)(2,1)} %get-tuple-element.112), calls=%async_computation | async-start | bytes 16777216 | tf_op jit(solution)/shard_map/all_to_all | solution.py:53
where the time goes:
time: 688 us; the launch traced here: 684 us
  local copies, waits for them, and re-layouts  239 us (35%)
  blocking collectives  193 us (28%)
  matrix products  187 us (27%)
  other arithmetic  57.9 us (8%)
    all_gather x1, blocking collectives, on_device(): power = lax.all_gather(input_power(scaled), 'chan', axis=0, tiled=True)  193 us
    reshape x16, local copies, waits for them, and re-layouts, select(): return picked.astype(jnp.bfloat16).reshape(group_size, PANEL, 2, half)  111 us
    dot_general x8, matrix products, one_group(): jnp.einsum('kiat,kjbt->kabij', left, right, preferred_element_type=jnp.fl...  100 us
    dot_general x16, matrix products, select(): jnp.einsum('kn,nix->kix', onehot, panels, preferred_element_type=jnp.floa...  86.8 us
    dynamic_update_slice x16, local copies, waits for them, and re-layouts, correlate_plane(): return lax.map(one_group, groups).reshape(-1, 2, PANEL, PANEL)  82.5 us
    dynamic_update_slice x2, local copies, waits for them, and re-layouts, correlate_channels(): return lax.map(one_channel, jnp.moveaxis(turned, 1, 0))  23.3 us
    convert_element_type x1, other arithmetic, on_device(): return (raw / denom[None, :, None, :, :]).astype(jnp.bfloat16)  19.9 us
    broadcast_in_dim x8, other arithmetic, correlate_plane(): return lax.map(one_group, groups).reshape(-1, 2, PANEL, PANEL)  18 us
  transfers between devices with their start and end apart: 1, of which 0 were waited for; matrix products, arithmetic and copies ran while one was open for 1% of the time, Pallas kernels for 0%

commit v1 on v0

--- a/solution.py
+++ b/solution.py
@@ -5,6 +5,19 @@
 
 PANEL = 128
 NT = 256
+
+
+def ring_gather(shard, axis, dim):
+    size, index, rows = (lax.axis_size(axis), lax.axis_index(axis), shard.shape[dim])
+    upward = [(i, (i + 1) % size) for i in range(size)]
+    out = jnp.zeros((*shard.shape[:dim], size * rows, *shard.shape[dim + 1 :]), shard.dtype)
+    current = shard
+    for lap in range(size):
+        owner = (index - lap) % size
+        out = lax.dynamic_update_slice_in_dim(out, current, owner * rows, axis=dim)
+        if lap < size - 1:
+            current = lax.ppermute(current, axis, upward)
+    return out
 
 
 def correlate_plane(plane, pairs):
@@ -49,7 +62,7 @@
     gain = jnp.exp2(-exponents.astype(jnp.float32)).astype(jnp.bfloat16)
     scaled = voltages * gain[None, :, None]
     total_samples = exponents.shape[0] * NT
-    power = lax.all_gather(input_power(scaled), "chan", axis=0, tiled=True)
+    power = ring_gather(input_power(scaled), "chan", 0)
     turned = lax.all_to_all(scaled, "chan", split_axis=1, concat_axis=0, tiled=True)
     raw = correlate_channels(turned, pairs)
     mean_power = power / total_samples

time: 688 us -> 733 us (1.065)
  blocking collectives: 193 us -> 0 us
  waiting for transfers between devices: 0.01 us -> 144 us
  starting transfers between devices: 6.74 us -> 92.1 us
    all_gather x1 -> x0, blocking collectives: 193 us -> none  [on_device(): power = lax.all_gather(input_power(scaled), 'chan', axis=0, tiled=True)]
    ppermute x0 -> x15, waiting for transfers between devices: none -> 144 us  [ring_gather(): current = lax.ppermute(current, axis, upward)]
    ppermute x0 -> x15, starting transfers between devices: none -> 85.3 us  [ring_gather(): current = lax.ppermute(current, axis, upward)]
  transfers between devices with their start and end apart: 1 -> 16, of which waited for: 0 -> 14; matrix products, arithmetic and copies ran while one was open for 1% -> 1% of each run, Pallas kernels for 0% -> 0%
where the time goes in v1:
time: 733 us; the launch traced here: 724 us
  local copies, waits for them, and re-layouts  243 us (33%)
  matrix products  187 us (26%)
  waiting for transfers between devices  144 us (20%)
  starting transfers between devices  92.1 us (13%)
  other arithmetic  58.1 us (8%)
    ppermute x15, waiting for transfers between devices, ring_gather(): current = lax.ppermute(current, axis, upward)  144 us
    reshape x16, local copies, waits for them, and re-layouts, select(): return picked.astype(jnp.bfloat16).reshape(group_size, PANEL, 2, half)  111 us
    dot_general x8, matrix products, one_group(): jnp.einsum('kiat,kjbt->kabij', left, right, preferred_element_type=jnp.fl...  100 us
    dot_general x16, matrix products, select(): jnp.einsum('kn,nix->kix', onehot, panels, preferred_element_type=jnp.floa...  86.9 us
    ppermute x15, starting transfers between devices, ring_gather(): current = lax.ppermute(current, axis, upward)  85.3 us
    dynamic_update_slice x16, local copies, waits for them, and re-layouts, correlate_plane(): return lax.map(one_group, groups).reshape(-1, 2, PANEL, PANEL)  82.4 us
    dynamic_update_slice x2, local copies, waits for them, and re-layouts, correlate_channels(): return lax.map(one_channel, jnp.moveaxis(turned, 1, 0))  23.3 us
    convert_element_type x1, other arithmetic, on_device(): return (raw / denom[None, :, None, :, :]).astype(jnp.bfloat16)  19.9 us
  transfers between devices with their start and end apart: 16, of which 14 were waited for; matrix products, arithmetic and copies ran while one was open for 1% of the time, Pallas kernels for 0%

profile of v1, /device:TPU:11, one launch (start us, length us, event | category | flops | bytes accessed | tf_op | source)
XLA Modules:
  0.0 724.3 jit_solution(7984971219558250530)
XLA Ops:
  0.7 9.6 %multiply_reduce_fusion = (f32[256]{0:T(256)S(1)}, bf16[256,32,512]{2,0,1:T(8,128)(2,1)}) fusion(bf16[32]{0:T(256)(128)(2,1)S(1)} %exponential_convert_fusion, bf16[256,32,512]{2,1,0:T(8,128)(2,1)} %param.9), kind=kLoop, calls=%fused_computation.29 | loop fusion | flops 16776960 | bytes 16778304 | tf_op jit(solution)/shard_map/reduce_sum | solution.py:58
  10.3 6.7 all-to-all-start
  18.5 32.6 %collective-permute-done = f32[256]{0:T(256)S(1)} collective-permute-done((f32[256]{0:T(256)S(1)}, f32[256]{0:T(256)S(1)}, u32[]{:S(2)}, u32[]{:S(2)}) %collective-permute-start) | collective-permute-done | bytes 1056 | tf_op jit(solution)/shard_map/ppermute | solution.py:19
  53.5 102.7 %collective-permute-done.1 = f32[256]{0:T(256)S(1)} collective-permute-done((f32[256]{0:T(256)S(1)}, f32[256]{0:T(256)S(1)}, u32[]{:S(2)}, u32[]{:S(2)}) %collective-permute-start.1) | collective-permute-done | bytes 1056 | tf_op jit(solution)/shard_map/ppermute | solution.py:19
  156.2 43.4 %collective-permute-start.2 = (f32[256]{0:T(256)S(1)}, f32[256]{0:T(256)S(1)}, u32[]{:S(2)}, u32[]{:S(2)}) collective-permute-start(f32[256]{0:T(256)S(1)} %collective-permute-done.1), channel_id=1, source_target_pairs={{0,1},{1,2},{2,3},{3,4},{4,5},{5,6},{6,7},{7,8},{8,9},{9,10},{10,1... | collective-permute-start | bytes 3080 | tf_op jit(solution)/shard_map/ppermute | solution.py:19
  256.1 7.5 %copy.26 = bf16[16,256,2,512]{3,1,0,2:T(8,128)(2,1)} copy(bf16[16,256,2,512]{3,1,2,0:T(8,128)(2,1)} %bitcast.3) | data formatting | bytes 16777216 | tf_op jit(solution)/shard_map/all_to_all | solution.py:66
  263.5 440.8 %while.23 = (s32[]{:T(128)}, f32[2,128,2,128,128]{4,3,2,1,0:T(8,128)}, s32[128,2]{0,1:T(2,128)S(1)}, bf16[2,4096,512]{2,1,0:T(8,128)(2,1)}, s32[]{:T(128)}, /*index=5*/s32[]{:T(128)}, s32[]{:T(128)}) while((s32[]{:T(128)}, f32[2,128,2,128,128]{4,3,2,1,0:T(8,128)}, s32[128,2]{0,1:T(2,128)S(1)}, bf16[2,4096,512]{2,1,0:T(8,128)(2,1)}, s32[]{:T(128)}, ...), condition=%wide.region_3.4_spmd, body=%wide.region_0.3_spmd.sunk | while | flops 1348470784 | bytes 138415600 | solution.py:53
  270.5 201.8 %while.24 = (s32[]{:T(128)}, f32[4,32,2,128,128]{4,3,2,1,0:T(8,128)}, s32[4,32,2]{1,0,2:T(4,128)S(1)}, bf16[32,128,512]{2,0,1:T(8,128)(2,1)}, s32[]{:T(128)}) while((s32[]{:T(128)}, f32[4,32,2,128,128]{4,3,2,1,0:T(8,128)}, s32[4,32,2]{1,0,2:T(4,128)S(1)}, bf16[32,128,512]{2,0,1:T(8,128)(2,1)}, s32[]{:T(128)}) %tuple.52), condition=%wide.region_2.2_spmd.clone.clone, body=%wide.region_1.1_spmd.clone.clone.sunk | while | flops 1348470784 | bytes 88081744 | solution.py:45
  276.0 6.9 reshape.101
  288.3 6.9 reshape.102
  295.2 12.5 %fusion.36 = f32[32,2,2,128,128]{3,4,1,2,0:T(8,128)S(1)} fusion(bf16[32,128,2,256,1]{3,2,0,1,4:T(2,128)(2,1)} %bitcast.91, bf16[32,128,2,256,1]{3,2,0,1,4:T(2,128)(2,1)} %bitcast.92), kind=kOutput, calls=%fused_computation.7.clone.1 | convolution fusion | flops 1073741824 | bytes 16777216 | tf_op jit(solution)/shard_map/while/body/eval_jaxpr/while/body/eval_jaxpr/kiat,kjbt->kabij/dot_general | solution.py:40
  310.7 5.6 copy.55
  326.4 6.9 reshape.101
  338.8 6.9 reshape.102
  345.7 12.5 %fusion.36 = f32[32,2,2,128,128]{3,4,1,2,0:T(8,128)S(1)} fusion(bf16[32,128,2,256,1]{3,2,0,1,4:T(2,128)(2,1)} %bitcast.91, bf16[32,128,2,256,1]{3,2,0,1,4:T(2,128)(2,1)} %bitcast.92), kind=kOutput, calls=%fused_computation.7.clone.1 | convolution fusion | flops 1073741824 | bytes 16777216 | tf_op jit(solution)/shard_map/while/body/eval_jaxpr/while/body/eval_jaxpr/kiat,kjbt->kabij/dot_general | solution.py:40
  361.1 5.6 copy.55
  376.8 6.9 reshape.101
  383.8 5.5 convolution_convert_fusion.5
  389.2 6.9 reshape.102
  396.1 12.5 %fusion.36 = f32[32,2,2,128,128]{3,4,1,2,0:T(8,128)S(1)} fusion(bf16[32,128,2,256,1]{3,2,0,1,4:T(2,128)(2,1)} %bitcast.91, bf16[32,128,2,256,1]{3,2,0,1,4:T(2,128)(2,1)} %bitcast.92), kind=kOutput, calls=%fused_computation.7.clone.1 | convolution fusion | flops 1073741824 | bytes 16777216 | tf_op jit(solution)/shard_map/while/body/eval_jaxpr/while/body/eval_jaxpr/kiat,kjbt->kabij/dot_general | solution.py:40
  411.5 5.6 copy.55
  427.3 6.9 reshape.101
  434.2 5.5 convolution_convert_fusion.5
  439.7 6.9 reshape.102
  446.6 12.5 %fusion.36 = f32[32,2,2,128,128]{3,4,1,2,0:T(8,128)S(1)} fusion(bf16[32,128,2,256,1]{3,2,0,1,4:T(2,128)(2,1)} %bitcast.91, bf16[32,128,2,256,1]{3,2,0,1,4:T(2,128)(2,1)} %bitcast.92), kind=kOutput, calls=%fused_computation.7.clone.1 | convolution fusion | flops 1073741824 | bytes 16777216 | tf_op jit(solution)/shard_map/while/body/eval_jaxpr/while/body/eval_jaxpr/kiat,kjbt->kabij/dot_general | solution.py:40
  462.0 5.6 copy.55
  472.3 11.6 %bitcast_dynamic-update-slice_fusion.2 = f32[2,128,2,128,128]{4,3,2,1,0:T(8,128)} fusion(f32[2,128,2,128,128]{4,3,2,1,0:T(8,128)} %get-tuple-element.207, s32[]{:T(128)S(6)} %copy.66, f32[1,128,2,128,128]{4,3,2,1,0:T(8,128)} %bitcast.93), kind=kLoop, calls=%fused_computation.26.clone.1 | loop fusion | bytes 33554436 | tf_op jit(solution)/shard_map/while/body/jit(dynamic_update_index_in_dim)/dynamic_update_slice | solution.py:53
  490.9 201.8 %while.24 = (s32[]{:T(128)}, f32[4,32,2,128,128]{4,3,2,1,0:T(8,128)}, s32[4,32,2]{1,0,2:T(4,128)S(1)}, bf16[32,128,512]{2,0,1:T(8,128)(2,1)}, s32[]{:T(128)}) while((s32[]{:T(128)}, f32[4,32,2,128,128]{4,3,2,1,0:T(8,128)}, s32[4,32,2]{1,0,2:T(4,128)S(1)}, bf16[32,128,512]{2,0,1:T(8,128)(2,1)}, s32[]{:T(128)}) %tuple.52), condition=%wide.region_2.2_spmd.clone.clone, body=%wide.region_1.1_spmd.clone.clone.sunk | while | flops 1348470784 | bytes 88081744 | solution.py:45
  496.3 6.9 reshape.101
  503.3 5.5 convolution_convert_fusion.5
  508.8 6.9 reshape.102
  515.7 12.5 %fusion.36 = f32[32,2,2,128,128]{3,4,1,2,0:T(8,128)S(1)} fusion(bf16[32,128,2,256,1]{3,2,0,1,4:T(2,128)(2,1)} %bitcast.91, bf16[32,128,2,256,1]{3,2,0,1,4:T(2,128)(2,1)} %bitcast.92), kind=kOutput, calls=%fused_computation.7.clone.1 | convolution fusion | flops 1073741824 | bytes 16777216 | tf_op jit(solution)/shard_map/while/body/eval_jaxpr/while/body/eval_jaxpr/kiat,kjbt->kabij/dot_general | solution.py:40
  531.1 5.6 copy.55
  546.8 6.9 reshape.101
  553.7 5.5 convolution_convert_fusion.5
  559.2 6.9 reshape.102
  566.1 12.5 %fusion.36 = f32[32,2,2,128,128]{3,4,1,2,0:T(8,128)S(1)} fusion(bf16[32,128,2,256,1]{3,2,0,1,4:T(2,128)(2,1)} %bitcast.91, bf16[32,128,2,256,1]{3,2,0,1,4:T(2,128)(2,1)} %bitcast.92), kind=kOutput, calls=%fused_computation.7.clone.1 | convolution fusion | flops 1073741824 | bytes 16777216 | tf_op jit(solution)/shard_map/while/body/eval_jaxpr/while/body/eval_jaxpr/kiat,kjbt->kabij/dot_general | solution.py:40
  581.5 5.6 copy.55
  597.2 6.9 reshape.101
  609.6 6.9 reshape.102
  616.5 12.5 %fusion.36 = f32[32,2,2,128,128]{3,4,1,2,0:T(8,128)S(1)} fusion(bf16[32,128,2,256,1]{3,2,0,1,4:T(2,128)(2,1)} %bitcast.91, bf16[32,128,2,256,1]{3,2,0,1,4:T(2,128)(2,1)} %bitcast.92), kind=kOutput, calls=%fused_computation.7.clone.1 | convolution fusion | flops 1073741824 | bytes 16777216 | tf_op jit(solution)/shard_map/while/body/eval_jaxpr/while/body/eval_jaxpr/kiat,kjbt->kabij/dot_general | solution.py:40
  632.0 5.6 copy.55
  647.7 6.9 reshape.101
  660.1 6.9 reshape.102
  667.0 12.5 %fusion.36 = f32[32,2,2,128,128]{3,4,1,2,0:T(8,128)S(1)} fusion(bf16[32,128,2,256,1]{3,2,0,1,4:T(2,128)(2,1)} %bitcast.91, bf16[32,128,2,256,1]{3,2,0,1,4:T(2,128)(2,1)} %bitcast.92), kind=kOutput, calls=%fused_computation.7.clone.1 | convolution fusion | flops 1073741824 | bytes 16777216 | tf_op jit(solution)/shard_map/while/body/eval_jaxpr/while/body/eval_jaxpr/kiat,kjbt->kabij/dot_general | solution.py:40
  682.4 5.6 copy.55
  692.7 11.6 %bitcast_dynamic-update-slice_fusion.2 = f32[2,128,2,128,128]{4,3,2,1,0:T(8,128)} fusion(f32[2,128,2,128,128]{4,3,2,1,0:T(8,128)} %get-tuple-element.207, s32[]{:T(128)S(6)} %copy.66, f32[1,128,2,128,128]{4,3,2,1,0:T(8,128)} %bitcast.93), kind=kLoop, calls=%fused_computation.26.clone.1 | loop fusion | bytes 33554436 | tf_op jit(solution)/shard_map/while/body/jit(dynamic_update_index_in_dim)/dynamic_update_slice | solution.py:53
  704.3 19.9 %divide_convert_fusion = bf16[2,128,2,128,128]{4,3,2,1,0:T(8,128)(2,1)} fusion(f32[2,128,2,128,128]{4,3,2,1,0:T(8,128)} %get-tuple-element.58, f32[128,128,128]{2,1,0:T(8,128)} %multiply_sqrt_fusion), kind=kLoop, calls=%fused_computation.28 | loop fusion | flops 16777216 | bytes 58720256 | tf_op jit(solution)/shard_map/convert_element_type | solution.py:73
  (125 shorter events, 200.7 us)
Async XLA Ops:
  10.3 8.2 %copy-start = (s32[128,2]{0,1:T(2,128)S(1)}, s32[128,2]{0,1:T(2,128)}, u32[]{:S(2)}) copy-start(s32[128,2]{0,1:T(2,128)} %param.11) | copy-start | bytes 3076
  10.3 245.8 %all-to-all-start = ((bf16[256,32,512]{2,0,1:T(8,128)(2,1)}), bf16[256,32,512]{2,0,1:T(8,128)(2,1)}, u32[]{:S(2)}, u32[]{:S(2)}) async-start(bf16[256,32,512]{2,0,1:T(8,128)(2,1)} %get-tuple-element.112), calls=%async_computation | async-start | bytes 16777216 | tf_op jit(solution)/shard_map/all_to_all | solution.py:66
  17.0 34.0 %collective-permute-start = (f32[256]{0:T(256)S(1)}, f32[256]{0:T(256)S(1)}, u32[]{:S(2)}, u32[]{:S(2)}) collective-permute-start(f32[256]{0:T(256)S(1)} %get-tuple-element.111), channel_id=1, source_target_pairs={{0,1},{1,2},{2,3},{3,4},{4,5},{5,6},{6,7},{7,8},{8,9},{9,10},{10,1... | collective-permute-start | bytes 3080 | tf_op jit(solution)/shard_map/ppermute | solution.py:19
  51.1 105.1 %collective-permute-start.1 = (f32[256]{0:T(256)S(1)}, f32[256]{0:T(256)S(1)}, u32[]{:S(2)}, u32[]{:S(2)}) collective-permute-start(f32[256]{0:T(256)S(1)} %collective-permute-done), channel_id=1, source_target_pairs={{0,1},{1,2},{2,3},{3,4},{4,5},{5,6},{6,7},{7,8},{8,9},{9,10},{10,1... | collective-permute-start | bytes 3080 | tf_op jit(solution)/shard_map/ppermute | solution.py:19
  156.2 44.1 %collective-permute-start.2 = (f32[256]{0:T(256)S(1)}, f32[256]{0:T(256)S(1)}, u32[]{:S(2)}, u32[]{:S(2)}) collective-permute-start(f32[256]{0:T(256)S(1)} %collective-permute-done.1), channel_id=1, source_target_pairs={{0,1},{1,2},{2,3},{3,4},{4,5},{5,6},{6,7},{7,8},{8,9},{9,10},{10,1... | collective-permute-start | bytes 3080 | tf_op jit(solution)/shard_map/ppermute | solution.py:19
  200.3 4.0 collective-permute-start.3
  204.3 3.9 collective-permute-start.4
  208.2 3.9 collective-permute-start.5
  212.1 3.9 collective-permute-start.6
  216.0 3.9 collective-permute-start.7
  219.9 3.9 collective-permute-start.8
  223.8 3.9 collective-permute-start.9
  227.7 3.9 collective-permute-start.10
  231.6 3.9 collective-permute-start.11
  235.5 3.9 collective-permute-start.12
  239.4 3.9 collective-permute-start.13
  243.3 6.5 collective-permute-start.14
